TPU v7x, 32 devices: a whole 2x2x4 slice. The times are simulated.
32 devices in a mesh: pair: 8 (over z, x), vir: 4 (over y, core).
Axes of the slice: x: 2, y: 2, z: 4, core: 2. Of those that a mesh axis runs over, the one named last changes fastest.
Arguments:
- amplitudes: float32 [3072, 4096], P(('pair', 'vir')), may hold values from -6 to 6
- integrals: float32 [1536, 1536], P('vir'), may hold values from -0.15625 to 0.15625
- tile_owner: int32 [3072], P(('pair', 'vir')), may hold values from 0 to 7, as said below
- tile_key: int32 [3072], P(('pair', 'vir')), may hold values from 0 to 575
Outputs:
- residual: float32 [3072, 4096], P(('pair', 'vir'))
Inputs may be any that keep to these rules, and one draw needn't show every extreme that they name: `tile_owner`: among the 96 tiles of one device no owner is named more than 24 times; one owner, the same for every device, is named exactly 24 times by each device.
All inputs are finite; a program needn't handle non-finite values.
Results may differ from a plain program's by a relative error of at most 0.0003.
Values sent between devices are 32-bit elements; how exact they have to be, the bound alone decides.
A program may use at most 128 MiB of HBM per device.

v0:
```python
import jax
import jax.numpy as jnp
from jax import lax
from jax.sharding import PartitionSpec as P

TS = 64
NS = 24
ROWSETS_DEV = 24


def per_device(amplitudes, integrals, tile_owner, tile_key):
    owner_count = lax.axis_size("pair")
    capacity = max(2, 2 * amplitudes.shape[0] // owner_count)
    picked = (tile_owner[:, None] == jnp.arange(owner_count, dtype=jnp.int32)[None, :]).astype(
        jnp.int32
    )
    before = jnp.cumsum(picked, axis=0) - picked
    slot_index = jnp.sum(before * picked, axis=1)
    send_tiles = (
        jnp.zeros((owner_count, capacity, TS * TS), jnp.float32)
        .at[tile_owner, slot_index]
        .set(amplitudes)
    )
    send_keys = (
        jnp.zeros((owner_count, capacity), jnp.int32).at[tile_owner, slot_index].set(tile_key)
    )
    recv_tiles, recv_keys = (
        lax.all_to_all(send_tiles, "pair", split_axis=0, concat_axis=0, tiled=True),
        lax.all_to_all(send_keys, "pair", split_axis=0, concat_axis=0, tiled=True),
    )
    arrived = recv_tiles.reshape(owner_count * capacity, TS, TS)
    flat_keys = recv_keys.reshape(owner_count * capacity)
    row_block = flat_keys // NS
    col_block = flat_keys % NS
    blocked = (
        jnp.zeros((ROWSETS_DEV, TS, NS, TS), jnp.float32)
        .at[row_block, :, col_block, :]
        .add(arrived)
    )
    blocked = blocked.reshape(ROWSETS_DEV * TS, NS * TS)
    product = jnp.dot(
        blocked,
        lax.all_gather(integrals, "vir", axis=0, tiled=True),
        precision=lax.Precision.HIGHEST,
        preferred_element_type=jnp.float32,
    )
    product = product.reshape(ROWSETS_DEV, TS, NS, TS)
    answers = product[row_block, :, col_block, :].reshape(owner_count, capacity, TS * TS)
    returned = lax.all_to_all(answers, "pair", split_axis=0, concat_axis=0, tiled=True)
    return returned[tile_owner, slot_index]


def solution(mesh):
    placed = (P(("pair", "vir"), None), P("vir", None), P(("pair", "vir")), P(("pair", "vir")))
    return jax.shard_map(
        per_device, mesh=mesh, in_specs=placed, out_specs=P(("pair", "vir"), None), check_vma=False
    )
```

profile of v0, /device:TPU:0, one launch (start us, length us, event | category | flops | bytes accessed | tf_op | source)
XLA Modules:
  0.0 422.6 jit_solution(8171510765054190100)
XLA Ops:
  6.5 0.0 copy-start
  6.5 0.0 all-gather.2.cloned.1.call-start
  6.5 0.7 all-gather.2.cloned.1.call-update
  7.3 0.7 fusion.2
  8.0 0.1 reduce_window_sum.11
  8.1 0.8 select_reduce_fusion
  9.0 0.7 fusion.7
  9.6 0.6 broadcast_in_dim.9
  10.2 15.0 %scatter_fusion = s32[8,24]{1,0:T(8,128)} fusion(s32[8,24]{1,0:T(8,128)} %broadcast_in_dim.9, s32[96]{0:T(128)S(1)} %get-tuple-element.11, s32[96]{0:T(128)} %param.7), kind=kCustom, calls=%fused_computation.2 | custom fusion | bytes 1920 | tf_op jit(solution)/shard_map/scatter | solution.py:25
  25.3 7.3 %all-to-all-start = ((s32[8,1,24]{2,1,0:T(1,128)}), s32[8,1,24]{2,1,0:T(1,128)S(1)}, u32[]{:S(2)}, u32[]{:S(2)}) async-start(s32[8,1,24]{2,1,0:T(1,128)} %bitcast.4), calls=%async_computation | async-start | bytes 8192 | tf_op jit(solution)/shard_map/all_to_all | solution.py:29
  32.5 2.0 broadcast_in_dim.11
  34.5 0.0 copy-done
  34.5 23.5 %scatter_fusion.1 = f32[8,24,4096]{2,1,0:T(8,128)} fusion(f32[8,24,4096]{2,1,0:T(8,128)} %broadcast_in_dim.11, s32[96]{0:T(128)S(1)} %get-tuple-element.11, f32[96,4096]{1,0:T(8,128)S(1)} %copy-done), kind=kCustom, calls=%fused_computation.3 | custom fusion | bytes 4719360 | tf_op jit(solution)/shard_map/scatter | solution.py:22
  58.0 0.0 all-to-all-done
  58.0 6.5 %all-to-all-start.1 = ((f32[8,24,4096]{2,1,0:T(8,128)}), f32[8,24,4096]{2,1,0:T(8,128)S(1)}, u32[]{:S(2)}, u32[]{:S(2)}) async-start(f32[8,24,4096]{2,1,0:T(8,128)} %scatter_fusion.1), calls=%async_computation.1 | async-start | bytes 6291456 | tf_op jit(solution)/shard_map/all_to_all | solution.py:28
  64.5 0.1 div.17
  64.6 0.1 rem.30
  64.7 0.1 ne.52
  64.8 69.4 %all-to-all-done.1 = f32[8,24,4096]{2,1,0:T(8,128)S(1)} async-done(((f32[8,24,4096]{2,1,0:T(8,128)}), f32[8,24,4096]{2,1,0:T(8,128)S(1)}, u32[]{:S(2)}, u32[]{:S(2)}) %all-to-all-start.1) | async-done | bytes 3145760 | tf_op jit(solution)/shard_map/all_to_all | solution.py:28
  134.2 4.2 %reshape.142 = f32[192,64,64]{2,1,0:T(8,128)} reshape(f32[8,24,4096]{2,1,0:T(8,128)S(1)} %all-to-all-done.1) | data formatting | bytes 6291456 | tf_op jit(solution)/shard_map/reshape | solution.py:31
  138.4 9.0 %broadcast_in_dim.8 = f32[24,64,24,64]{3,1,2,0:T(8,128)} broadcast(f32[]{:T(128)} %constant.16.clone.1), dimensions={} | broadcast | bytes 9437188 | tf_op jit(solution)/shard_map/broadcast_in_dim | solution.py:36
  147.4 31.6 %scatter_fusion.2 = f32[24,64,24,64]{3,1,2,0:T(8,128)} fusion(f32[24,64,24,64]{3,1,2,0:T(8,128)} %broadcast_in_dim.8, s32[192]{0:T(256)S(1)} %bitcast.39, f32[192,64,64]{2,1,0:T(8,128)} %reshape.142), kind=kCustom, calls=%fused_computation.4 | custom fusion | flops 786432 | bytes 9438720 | tf_op jit(solution)/shard_map/scatter-add | solution.py:38
  179.0 19.8 %copy.12 = f32[24,64,24,64]{3,2,1,0:T(8,128)} copy(f32[24,64,24,64]{3,1,2,0:T(8,128)} %scatter_fusion.2) | data formatting | bytes 18874368 | tf_op jit(solution)/shard_map/scatter-add | solution.py:38
  198.8 16.3 %reshape.146 = f32[24,64,1536,1]{2,1,0,3:T(8,128)} reshape(f32[24,64,24,64]{3,2,1,0:T(8,128)} %copy.12) | data formatting | bytes 18874368 | tf_op jit(solution)/shard_map/dot_general | solution.py:41
  215.1 0.0 all-gather.2.cloned.1.call-done
  215.1 9.6 %copy.13 = f32[1536,1536]{1,0:T(8,128)} copy(f32[1536,1536]{0,1:T(8,128)} %bitcast.41) | data formatting | bytes 18874368 | tf_op jit(solution)/shard_map/dot_general | solution.py:41
  224.8 95.6 %fusion = f32[24,64,24,64]{3,1,2,0:T(8,128)} fusion(f32[24,64,1536,1]{2,1,0,3:T(8,128)} %bitcast.42, f32[24,64,1536,1]{2,1,0,3:T(8,128)} %reshape.146), kind=kOutput, calls=%fused_computation.5 | convolution fusion | flops 43486543872 | bytes 28311552 | tf_op jit(solution)/shard_map/dot_general | solution.py:41
  320.3 10.8 %gather_fusion = f32[192,64,64]{2,1,0:T(8,128)} fusion(f32[24,64,24,64]{3,1,2,0:T(8,128)} %fusion, s32[192]{0:T(256)S(1)} %bitcast.40), kind=kCustom, calls=%fused_computation | custom fusion | bytes 6292992 | tf_op jit(solution)/shard_map/gather | solution.py:48
  331.1 5.9 %reshape.115 = f32[8,24,4096]{2,1,0:T(8,128)} reshape(f32[192,64,64]{2,1,0:T(8,128)} %gather_fusion) | data formatting | bytes 6291456 | tf_op jit(solution)/shard_map/reshape | solution.py:48
  337.1 74.5 %all_to_all.19 = f32[8,24,4096]{2,1,0:T(8,128)S(1)} all-to-all(f32[8,24,4096]{2,1,0:T(8,128)} %reshape.115), channel_id=1, replica_groups=mesh['pair'=8,'vir'=4] {'pair'}, dimensions={0} | all-to-all | bytes 6291456 | tf_op jit(solution)/shard_map/all_to_all | solution.py:49
  411.6 4.2 gather_fusion.1
  (4 shorter events, 0.1 us)
Async XLA Ops:
  6.5 28.0 %copy-start = (f32[96,4096]{1,0:T(8,128)S(1)}, f32[96,4096]{1,0:T(8,128)}, u32[]{:S(2)}) copy-start(f32[96,4096]{1,0:T(8,128)} %param.4) | copy-start | bytes 4718596
  6.5 208.6 %all-gather.2.cloned.1.call-start = ((), (), s32[]{:S(2)}) async-start(), calls=%async_computation.3 | async-start | bytes 11796480 | tf_op jit(solution)/shard_map/all_gather | solution.py:43
  25.3 32.7 %all-to-all-start = ((s32[8,1,24]{2,1,0:T(1,128)}), s32[8,1,24]{2,1,0:T(1,128)S(1)}, u32[]{:S(2)}, u32[]{:S(2)}) async-start(s32[8,1,24]{2,1,0:T(1,128)} %bitcast.4), calls=%async_computation | async-start | bytes 8192 | tf_op jit(solution)/shard_map/all_to_all | solution.py:29
  58.0 76.2 %all-to-all-start.1 = ((f32[8,24,4096]{2,1,0:T(8,128)}), f32[8,24,4096]{2,1,0:T(8,128)S(1)}, u32[]{:S(2)}, u32[]{:S(2)}) async-start(f32[8,24,4096]{2,1,0:T(8,128)} %scatter_fusion.1), calls=%async_computation.1 | async-start | bytes 6291456 | tf_op jit(solution)/shard_map/all_to_all | solution.py:28
Sparse Core Ops, SparseCore 0:
  8.9 66.9 all-gather.1
where the time goes:
time: 424 us; the launch traced here: 423 us
  local copies, waits for them, and re-layouts  121 us (29%)
  matrix products  95.6 us (23%)
  blocking collectives  74.5 us (18%)
  waiting for transfers between devices  70.1 us (17%)
  other arithmetic  34.1 us (8%)
  starting transfers between devices  13.7 us (3%)
  between operations  13.4 us (3%)
    dot_general x1, matrix products, per_device(): jnp.dot(blocked, lax.all_gather(integrals, 'vir', axis=0, tiled=True), pr...  95.6 us
    all_to_all x1, blocking collectives, per_device(): lax.all_to_all(answers, 'pair', split_axis=0, concat_axis=0, tiled=True)  74.5 us
    all_to_all x1, waiting for transfers between devices, per_device(): lax.all_to_all(send_tiles, 'pair', split_axis=0, concat_axis=0, tiled=True)  69.4 us
    scatter-add x1, other arithmetic, per_device(): blocked = jnp.zeros((ROWSETS_DEV, TS, NS, TS), jnp.float32).at[row_block,...  31.6 us
    dot_general x2, local copies, waits for them, and re-layouts, per_device(): jnp.dot(blocked, lax.all_gather(integrals, 'vir', axis=0, tiled=True), pr...  26 us
    scatter x1, local copies, waits for them, and re-layouts, per_device(): send_tiles = jnp.zeros((owner_count, capacity, TS * TS), jnp.float32).at[...  23.5 us
    scatter-add x1, local copies, waits for them, and re-layouts, per_device(): blocked = jnp.zeros((ROWSETS_DEV, TS, NS, TS), jnp.float32).at[row_block,...  19.8 us
    scatter x1, local copies, waits for them, and re-layouts, per_device(): jnp.zeros((owner_count, capacity), jnp.int32).at[tile_owner, slot_index]  15 us
  transfers between devices with their start and end apart: 3, of which 1 were waited for; matrix products, arithmetic and copies ran while one was open for 30% of the time, Pallas kernels for 0%

commit v1 on v0

v1 whole, which is shorter than its diff:
```python
import functools

import jax
import jax.numpy as jnp
from jax import lax
from jax.experimental import pallas as pl
from jax.experimental.pallas import tpu as pltpu
from jax.sharding import PartitionSpec as P

TS = 64
NS = 24
CHUNK = 4
UNROLL = 4
BLOCK = 768
HALF = TS // 2
LANES = 2 * TS


def product_kernel(
    unit_ref, ustart_ref, start_ref, count_ref, home_ref, order_ref, total_ref,
    tiles_ref, high_ref, low_ref, out_ref,
):
    left = lax.broadcasted_iota(jnp.int32, (HALF, LANES), 1) < TS

    @pl.when(pl.program_id(0) == 0)
    def _():
        out_ref[...] = jnp.zeros_like(out_ref)

    def one_unit(u):
        t = unit_ref[0, 0, u]
        base = start_ref[0, 0, t] + CHUNK * (u - ustart_ref[0, 0, t])
        valid = start_ref[0, 0, t] + count_ref[0, 0, t] - base
        column = home_ref[0, t]
        pair_block = column // 2
        tops, bottoms, highs, lows = [], [], [], []
        held = []
        for j in range(CHUNK):
            packed = order_ref[0, 0, base + j]
            p = packed // NS
            s = packed % NS
            tile = jnp.where(j < valid, tiles_ref[p], 0.0)
            held.append((tile, pltpu.roll(tile, TS, 1)))
            rows = pl.ds(pl.multiple_of(s * TS, TS), TS)
            highs.append(high_ref[pair_block, rows, :])
            lows.append(low_ref[pair_block, rows, :])
        for j in range(0, CHUNK, 2):
            (first, first_r), (second, second_r) = held[j], held[j + 1]
            tops.append(jnp.where(left, first, second_r))
            bottoms.append(jnp.where(left, first_r, second))
        lhs = jnp.concatenate(
            [jnp.concatenate(tops, axis=1), jnp.concatenate(bottoms, axis=1)], axis=0
        )
        lhs_high = lhs.astype(jnp.bfloat16)
        lhs_low = (lhs - lhs_high.astype(jnp.float32)).astype(jnp.bfloat16)
        rhs_high = jnp.concatenate(highs, axis=0)
        rhs_low = jnp.concatenate(lows, axis=0)
        both = jnp.dot(
            jnp.concatenate([lhs_high, lhs_low], axis=0), rhs_high,
            preferred_element_type=jnp.float32,
        )
        got = both[:TS] + both[TS:] + jnp.dot(
            lhs_high, rhs_low, preferred_element_type=jnp.float32
        )
        top, bottom = got[:HALF], got[HALF:]
        odd = column % 2 == 1
        rolled = pltpu.roll(jnp.where(odd, top, bottom), TS, 1)
        return t, jnp.where(odd, jnp.where(left, rolled, bottom), jnp.where(left, top, rolled))

    def group(g, carry):
        made = [one_unit(g * UNROLL + i) for i in range(UNROLL)]
        for t, value in made:
            out_ref[t] += value
        return carry

    lax.fori_loop(0, (total_ref[0, 0, 0] + UNROLL - 1) // UNROLL, group, 0)


def product(tiles, ids, mine, high, low, capacity):
    targets = mine.shape[0]
    blocks = ids.shape[0] // BLOCK
    ids = ids.reshape(blocks, BLOCK)
    row = ids // NS
    own_row = mine // NS
    index = jnp.arange(BLOCK, dtype=jnp.int32)
    before = (row[:, :, None] > row[:, None, :]) | (
        (row[:, :, None] == row[:, None, :]) & (index[:, None] > index[None, :])
    )
    position = jnp.sum(before.astype(jnp.int32), axis=2)
    packed = index[None, :] * NS + ids % NS
    order = jnp.sum(
        jnp.where(position[:, None, :] == index[None, :, None], packed[:, None, :], 0), axis=2
    )
    order = jnp.pad(order, ((0, 0), (0, 128)))
    start = jnp.sum((row[:, None, :] < own_row[None, :, None]).astype(jnp.int32), axis=2)
    count = jnp.sum((row[:, None, :] == own_row[None, :, None]).astype(jnp.int32), axis=2)
    units = (count + CHUNK - 1) // CHUNK
    among = jnp.arange(targets, dtype=jnp.int32)
    ustart = jnp.sum(jnp.where(among[None, :, None] > among[None, None, :], units[:, None, :], 0), axis=2)
    total = jnp.sum(units, axis=1)
    most = targets * pl.cdiv(capacity * (BLOCK // targets), CHUNK)
    slot = jnp.arange(most + 128, dtype=jnp.int32)
    uend = ustart + units
    unit = jnp.minimum(
        jnp.sum((uend[:, :, None] <= slot[None, None, :]).astype(jnp.int32), axis=1), targets - 1
    )
    smem = lambda shape: pl.BlockSpec((1, 1) + shape, lambda b: (b, 0, 0), memory_space=pltpu.SMEM)
    whole = lambda shape: pl.BlockSpec(
        shape, lambda b: (0,) * len(shape), memory_space=pltpu.VMEM, pipeline_mode=pl.Buffered(1)
    )
    tables = [unit, ustart, start, count, None, order, total[:, None]]
    specs = [None if v is None else smem((v.shape[1],)) for v in tables]
    tables = [(mine % NS)[None, :] if v is None else v[:, None, :] for v in tables]
    specs[4] = pl.BlockSpec((1, targets), lambda b: (0, 0), memory_space=pltpu.SMEM)
    return pl.pallas_call(
        product_kernel,
        grid=(blocks,),
        out_shape=jax.ShapeDtypeStruct((targets, HALF, LANES), jnp.float32),
        in_specs=specs
        + [
            pl.BlockSpec(
                (BLOCK, HALF, LANES), lambda b: (b, 0, 0),
                pipeline_mode=pl.Buffered(1 if blocks == 1 else 2),
            ),
            whole(high.shape),
            whole(low.shape),
        ],
        out_specs=pl.BlockSpec((targets, HALF, LANES), lambda b: (0, 0, 0)),
        compiler_params=pltpu.CompilerParams(vmem_limit_bytes=(36 if blocks == 1 else 48) * 2**20),
    )(*tables, tiles, high, low)


def per_device(amplitudes, integrals, tile_owner, tile_key):
    targets = amplitudes.shape[0]
    mine = tile_owner * (NS * NS) + tile_key
    ids = lax.all_gather(mine, "pair", axis=0, tiled=True)
    whole = lax.all_gather(integrals, "vir", axis=0, tiled=True)
    tiles = lax.all_gather(
        amplitudes.reshape(targets, HALF, LANES), "pair", axis=0, tiled=True
    )
    whole = whole.reshape(NS * TS, NS // 2, LANES).transpose(1, 0, 2)
    rounded = lax.reduce_precision(whole, 8, 7)
    high = rounded.astype(jnp.bfloat16)
    low = (whole - rounded).astype(jnp.bfloat16)
    capacity = max(2, 2 * targets // lax.axis_size("pair"))
    out = product(tiles, ids, mine, high, low, capacity)
    return out.reshape(targets, TS * TS)


def solution(mesh):
    placed = (P(("pair", "vir"), None), P("vir", None), P(("pair", "vir")), P(("pair", "vir")))
    return jax.shard_map(
        per_device, mesh=mesh, in_specs=placed, out_specs=P(("pair", "vir"), None), check_vma=False
    )
```

time: 424 us -> 294 us (0.69)
  waiting for transfers between devices: 70.1 us -> 206 us
  local copies, waits for them, and re-layouts: 121 us -> 23.1 us
  matrix products: 95.6 us -> 0 us
  blocking collectives: 74.5 us -> 13.1 us
  Pallas kernels: 0 us -> 25.8 us
  other arithmetic: 34.1 us -> 13.1 us
  starting transfers between devices: 13.7 us -> 0.04 us
    all_gather x1 -> x2, waiting for transfers between devices: 0.01 us -> 206 us  [the longest x1 158 us: per_device(): lax.all_gather(amplitudes.reshape(targets, HALF, LANES), 'pair', axis=0,...]
    dot_general x1 -> x0, matrix products: 95.6 us -> none  [per_device(): jnp.dot(blocked, lax.all_gather(integrals, 'vir', axis=0, tiled=True), pr...]
    all_to_all x1 -> x0, blocking collectives: 74.5 us -> none  [per_device(): lax.all_to_all(answers, 'pair', split_axis=0, concat_axis=0, tiled=True)]
    all_to_all x2 -> x0, waiting for transfers between devices: 69.4 us -> none  [the longest x1 69.4 us: per_device(): lax.all_to_all(send_tiles, 'pair', split_axis=0, concat_axis=0, tiled=True)]
    scatter x2 -> x0, local copies, waits for them, and re-layouts: 38.5 us -> none  [the longest x1 23.5 us: per_device(): send_tiles = jnp.zeros((owner_count, capacity, TS * TS), jnp.float32).at[...]
    scatter-add x1 -> x0, other arithmetic: 31.6 us -> none  [per_device(): blocked = jnp.zeros((ROWSETS_DEV, TS, NS, TS), jnp.float32).at[row_block,...]
    dot_general x2 -> x0, local copies, waits for them, and re-layouts: 26 us -> none  [per_device(): jnp.dot(blocked, lax.all_gather(integrals, 'vir', axis=0, tiled=True), pr...]
    pallas_call x0 -> x1, Pallas kernels: none -> 25.8 us  [product(): pl.pallas_call(product_kernel, grid=(blocks,), out_shape=jax.ShapeDtypeSt...]
  transfers between devices with their start and end apart: 3 -> 2, of which waited for: 1 -> 2; matrix products, arithmetic and copies ran while one was open for 30% -> 8% of each run, Pallas kernels for 0% -> 0%
where the time goes in v1:
time: 294 us; the launch traced here: 295 us
  waiting for transfers between devices  206 us (70%)
  Pallas kernels  25.8 us (9%)
  local copies, waits for them, and re-layouts  23.1 us (8%)
  between operations  14.1 us (5%)
  other arithmetic  13.1 us (4%)
  blocking collectives  13.1 us (4%)
    all_gather x1, waiting for transfers between devices, per_device(): lax.all_gather(amplitudes.reshape(targets, HALF, LANES), 'pair', axis=0,...  158 us
    all_gather x1, waiting for transfers between devices, per_device(): whole = lax.all_gather(integrals, 'vir', axis=0, tiled=True)  47.5 us
    pallas_call x1, Pallas kernels, product(): pl.pallas_call(product_kernel, grid=(blocks,), out_shape=jax.ShapeDtypeSt...  25.8 us
    unnamed x17, local copies, waits for them, and re-layouts  13.4 us
    unnamed x1, blocking collectives  13.1 us
    convert_element_type x1, other arithmetic, per_device(): low = (whole - rounded).astype(jnp.bfloat16)  10.8 us
    reshape x1, local copies, waits for them, and re-layouts, per_device(): whole = whole.reshape(NS * TS, NS // 2, LANES).transpose(1, 0, 2)  9.66 us
  transfers between devices with their start and end apart: 2, of which 2 were waited for; matrix products, arithmetic and copies ran while one was open for 8% of the time, Pallas kernels for 0%

profile of v1, /device:TPU:0, one launch (start us, length us, event | category | flops | bytes accessed | tf_op | source)
XLA Modules:
  0.0 294.9 jit_solution(1815951970351900017)
XLA Ops:
  6.5 0.0 all-gather.5.cloned.1.call-start
  6.5 3.1 %copy.9 = f32[384,1536]{0,1:T(8,128)} copy(f32[384,1536]{1,0:T(8,128)} %param.5) | data formatting | bytes 4718592 | tf_op args[1]
  9.6 0.0 copy-start.2
  9.6 0.0 all-gather.5.cloned.1.call-update
  9.7 0.0 all-gather.3.cloned.1.call-start
  9.7 1.3 copy-done.2
  11.0 0.0 copy-start.5
  11.0 0.0 copy-start.3
  11.0 0.0 copy-start.4
  11.0 1.4 copy.11
  12.5 0.0 all-gather.3.cloned.1.call-update
  12.5 0.0 copy-done.5
  12.5 0.6 dynamic-slice
  13.8 0.0 copy-done.3
  13.8 0.0 copy-done.4
  13.8 0.1 fusion.5
  13.9 13.1 %all-reduce.1 = s32[768]{0:T(1024)S(1)} all-reduce(s32[768]{0:T(1024)S(1)} %get-tuple-element.15), channel_id=1, replica_groups=mesh['pair'=8,'vir'=4] {'pair'}, use_global_device_ids=true, to_apply=%add.1 | all-reduce | flops 768 | bytes 6144
  27.0 0.2 convert_reduce_fusion.2
  27.2 0.7 fusion.7
  27.9 0.1 select_reduce_fusion.1
  28.0 0.3 convert_reduce_fusion.1
  28.4 0.5 convert_reduce_fusion
  28.9 0.3 select_reduce_fusion
  29.2 47.5 %all-gather.5.cloned.1.call-done = f32[1536,1536]{0,1:T(8,128)} async-done(((f32[384,1536]{0,1:T(8,128)}), f32[1536,1536]{0,1:T(8,128)}) %all-gather.5.cloned.1.call-update) | async-done | bytes 9437200 | tf_op jit(solution)/shard_map/all_gather | solution.py:136
  76.8 9.7 %copy.10 = f32[1536,12,128]{2,0,1:T(8,128)} copy(f32[1536,12,128]{0,2,1:T(8,128)} %bitcast.23) | data formatting | bytes 18874368 | tf_op jit(solution)/shard_map/reshape | solution.py:140
  86.4 10.8 %fusion = (bf16[12,1536,128]{2,1,0:T(8,128)(2,1)}, bf16[12,1536,128]{2,1,0:T(8,128)(2,1)}) fusion(f32[1536,12,128]{2,0,1:T(8,128)} %copy.10), kind=kLoop, calls=%fused_computation.2 | loop fusion | flops 9437184 | bytes 18874368 | tf_op jit(solution)/shard_map/convert_element_type | solution.py:143
  97.2 158.2 %all-gather.3.cloned.1.call-done.tiles_ref = f32[768,32,128]{2,1,0:T(8,128)} async-done(((f32[96,32,128]{2,1,0:T(8,128)}), f32[768,32,128]{2,1,0:T(8,128)}) %all-gather.3.cloned.1.call-update) | async-done | bytes 12582928 | tf_op jit(solution)/shard_map/all_gather | solution.py:137
  255.4 0.0 copy-start
  255.4 2.3 copy-done
  257.7 0.0 copy-start.1
  257.7 2.3 copy-done.1
  260.1 25.8 %shard_map.46 = f32[96,32,128]{2,1,0:T(8,128)S(1)} custom-call(s32[1,1,4736]{2,1,0:T(1,128)S(1)} %min.20.unit_ref, s32[1,1,96]{2,1,0:T(1,128)S(1)} %bitcast.22, s32[1,1,96]{2,1,0:T(1,128)S(1)} %bitcast.20, s32[1,1,96]{2,1,0:T(1,128)S(1)} %bitcast.21, s32[1,96]{1,0:T(1,128)S(1)} %get-tuple-element.13.home_ref, s32[1,1,896]{2,1,0:T(1,128)S(1)} %pad_bitcast_fusion.order_ref, ...), custom_call_target="tpu_custom_call" | custom-call | tf_op jit(solution)/shard_map/pallas_call | solution.py:114
  285.9 2.2 copy.14
  (7 shorter events, 0.1 us)
Async XLA Ops:
  6.5 70.2 %all-gather.5.cloned.1.call-start = ((), (), s32[]{:S(2)}) async-start(), calls=%async_computation.1 | async-start | bytes 11796480 | tf_op jit(solution)/shard_map/all_gather | solution.py:136
  9.6 1.4 copy-start.2
  9.7 245.8 %all-gather.3.cloned.1.call-start = ((), (), s32[]{:S(2)}) async-start(), calls=%async_computation | async-start | bytes 14155776 | tf_op jit(solution)/shard_map/all_gather | solution.py:137
  11.0 1.5 copy-start.5
  11.0 2.7 copy-start.3
  11.0 2.7 copy-start.4
  255.4 2.3 copy-start
  257.7 2.3 copy-start.1
Sparse Core Ops, SparseCore 0:
  9.8 66.9 all-gather.4
  78.9 176.4 all-gather.2

commit v2 on v1

--- a/solution.py
+++ b/solution.py
@@ -18,13 +18,24 @@
 
 def product_kernel(
     unit_ref, ustart_ref, start_ref, count_ref, home_ref, order_ref, total_ref,
-    tiles_ref, high_ref, low_ref, out_ref,
+    tiles_ref, whole_ref, out_ref, high_ref, low_ref,
 ):
     left = lax.broadcasted_iota(jnp.int32, (HALF, LANES), 1) < TS
 
     @pl.when(pl.program_id(0) == 0)
     def _():
         out_ref[...] = jnp.zeros_like(out_ref)
+
+        def split(i, carry):
+            rows = pl.ds(pl.multiple_of(i * TS, TS), TS)
+            for b in range(NS // 2):
+                value = whole_ref[b, rows, :]
+                rounded = value.astype(jnp.bfloat16)
+                high_ref[b, rows, :] = rounded
+                low_ref[b, rows, :] = (value - rounded.astype(jnp.float32)).astype(jnp.bfloat16)
+            return carry
+
+        lax.fori_loop(0, NS, split, 0)
 
     def one_unit(u):
         t = unit_ref[0, 0, u]
@@ -75,7 +86,7 @@
     lax.fori_loop(0, (total_ref[0, 0, 0] + UNROLL - 1) // UNROLL, group, 0)
 
 
-def product(tiles, ids, mine, high, low, capacity):
+def product(tiles, ids, mine, whole, capacity):
     targets = mine.shape[0]
     blocks = ids.shape[0] // BLOCK
     ids = ids.reshape(blocks, BLOCK)
@@ -104,9 +115,6 @@
         jnp.sum((uend[:, :, None] <= slot[None, None, :]).astype(jnp.int32), axis=1), targets - 1
     )
     smem = lambda shape: pl.BlockSpec((1, 1) + shape, lambda b: (b, 0, 0), memory_space=pltpu.SMEM)
-    whole = lambda shape: pl.BlockSpec(
-        shape, lambda b: (0,) * len(shape), memory_space=pltpu.VMEM, pipeline_mode=pl.Buffered(1)
-    )
     tables = [unit, ustart, start, count, None, order, total[:, None]]
     specs = [None if v is None else smem((v.shape[1],)) for v in tables]
     tables = [(mine % NS)[None, :] if v is None else v[:, None, :] for v in tables]
@@ -121,28 +129,260 @@
                 (BLOCK, HALF, LANES), lambda b: (b, 0, 0),
                 pipeline_mode=pl.Buffered(1 if blocks == 1 else 2),
             ),
-            whole(high.shape),
-            whole(low.shape),
+            pl.BlockSpec(whole.shape, lambda b: (0, 0, 0), pipeline_mode=pl.Buffered(1)),
         ],
         out_specs=pl.BlockSpec((targets, HALF, LANES), lambda b: (0, 0, 0)),
-        compiler_params=pltpu.CompilerParams(vmem_limit_bytes=(36 if blocks == 1 else 48) * 2**20),
-    )(*tables, tiles, high, low)
+        scratch_shapes=[pltpu.VMEM(whole.shape, jnp.bfloat16)] * 2,
+        compiler_params=pltpu.CompilerParams(vmem_limit_bytes=(40 if blocks == 1 else 54) * 2**20),
+    )(*tables, tiles, whole)
+
+
+MESH = pl.DeviceIdType.MESH
+PARTS = 6
+LINE = 4
+CROSS = PARTS - 1
+
+
+def gather_kernel(
+    tiles_ref, ints_ref, ids_ref, all_ref, whole_ref, allids_ref,
+    up_sem, down_sem, over_sem, recv_sem, ids_send, ids_recv, ints_send, ints_recv, local_sem,
+):
+    pair = lax.axis_index("pair")
+    vir = lax.axis_index("vir")
+    z, x = pair // 2, pair % 2
+    other = pair + 1 - 2 * x
+    sibling = vir + 1 - 2 * (vir % 2)
+    across = lax.rem(vir + 2, 4)
+    depth = ints_ref.shape[1]
+
+    barrier = pltpu.get_barrier_semaphore()
+    for k in range(1, 2 * LINE):
+        pl.semaphore_signal(
+            barrier, inc=1, device_id={"pair": lax.rem(pair + k, 2 * LINE)}, device_id_type=MESH
+        )
+    for peer in (sibling, across):
+        pl.semaphore_signal(barrier, inc=1, device_id={"vir": peer}, device_id_type=MESH)
+    pl.semaphore_wait(barrier, 2 * LINE + 1)
+
+    def id_copy(k):
+        return pltpu.make_async_remote_copy(
+            src_ref=ids_ref, dst_ref=allids_ref.at[pair], send_sem=ids_send.at[k - 1],
+            recv_sem=ids_recv.at[k - 1], device_id={"pair": lax.rem(pair + k, 2 * LINE)},
+            device_id_type=MESH,
+        )
+
+    def id_arrival(k):
+        source = lax.rem(pair + 2 * LINE - k, 2 * LINE)
+        return pltpu.make_async_remote_copy(
+            src_ref=ids_ref, dst_ref=allids_ref.at[source], send_sem=ids_send.at[k - 1],
+            recv_sem=ids_recv.at[k - 1], device_id={"pair": source}, device_id_type=MESH,
+        )
+
+    def tile_copy(ref, source, part, sems, peer):
+        return pltpu.make_async_remote_copy(
+            src_ref=ref, dst_ref=all_ref.at[source, part], send_sem=sems.at[source, part],
+            recv_sem=recv_sem.at[source, part], device_id={"pair": peer}, device_id_type=MESH,
+        )
+
+    def up(ref, source, part):
+        return tile_copy(ref, source, part, up_sem, pair + 2)
+
+    def down(ref, source, part):
+        return tile_copy(ref, source, part, down_sem, pair - 2)
+
+    def over(ref, source, part):
+        return tile_copy(ref, source, part, over_sem, other)
+
+    def arrive(source, part):
+        over(all_ref.at[source, part], source, part).wait_recv()
+
+    def ints_copy(ref, owner, index, peer):
+        rows = pl.ds(pl.multiple_of(owner * depth, depth), depth)
+        return pltpu.make_async_remote_copy(
+            src_ref=ref, dst_ref=whole_ref.at[:, rows, :], send_sem=ints_send.at[index],
+            recv_sem=ints_recv.at[index], device_id={"vir": peer}, device_id_type=MESH,
+        )
+
+    def rows_of(owner):
+        return whole_ref.at[:, pl.ds(pl.multiple_of(owner * depth, depth), depth), :]
+
+    for k in range(1, 2 * LINE):
+        id_copy(k).start()
+
+    over(tiles_ref.at[CROSS], pair, CROSS).start()
+
+    def own(part, carry):
+        @pl.when(z < LINE - 1)
+        def _():
+            up(tiles_ref.at[part], pair, part).start()
+
+        @pl.when(z > 0)
+        def _():
+            down(tiles_ref.at[part], pair, part).start()
+
+        @pl.when(part < CROSS)
+        def _():
+            over(tiles_ref.at[part], pair, part).start()
+
+        return carry
+
+    lax.fori_loop(0, PARTS, own, 0)
+    ints_copy(ints_ref, vir, 0, across).start()
+    ints_copy(ints_ref, vir, 1, sibling).start()
+    locals_ = [
+        pltpu.make_async_copy(tiles_ref, all_ref.at[pair], local_sem.at[0]),
+        pltpu.make_async_copy(ints_ref, rows_of(vir), local_sem.at[1]),
+        pltpu.make_async_copy(ids_ref, allids_ref.at[pair], local_sem.at[2]),
+    ]
+    for copy in locals_:
+        copy.start()
+
+    def from_below(distance, column, part, crosses):
+        source = (z - distance) * 2 + column
+
+        @pl.when(z >= distance)
+        def _():
+            arrive(source, part)
+
+            @pl.when(z < LINE - 1)
+            def _():
+                up(all_ref.at[source, part], source, part).start()
+
+            if crosses:
+                over(all_ref.at[source, part], source, part).start()
+
+    def from_above(distance, column, part, crosses):
+        source = (z + distance) * 2 + column
+
+        @pl.when(z + distance < LINE)
+        def _():
+            arrive(source, part)
+
+            @pl.when(z > 0)
+            def _():
+                down(all_ref.at[source, part], source, part).start()
+
+            if crosses:
+                over(all_ref.at[source, part], source, part).start()
+
+    for distance in range(1, LINE):
+
+        def step(part, carry, distance=distance):
+            from_below(distance, x, part, True)
+            from_above(distance, x, part, True)
+            return carry
+
+        lax.fori_loop(0, CROSS, step, 0)
+        from_below(distance, x, CROSS, False)
+        from_above(distance, x, CROSS, False)
+        if distance == 1:
+            arrive(other, CROSS)
+
+            @pl.when(z < LINE - 1)
+            def _():
+                up(all_ref.at[other, CROSS], other, CROSS).start()
+
+            @pl.when(z > 0)
+            def _():
+                down(all_ref.at[other, CROSS], other, CROSS).start()
+
+        else:
+            from_below(distance - 1, 1 - x, CROSS, False)
+            from_above(distance - 1, 1 - x, CROSS, False)
+        if distance == 2:
+            ints_copy(rows_of(across), across, 0, across).wait_recv()
+            ints_copy(rows_of(across), across, 2, sibling).start()
+    from_below(LINE - 1, 1 - x, CROSS, False)
+    from_above(LINE - 1, 1 - x, CROSS, False)
+
+    def last(part, carry):
+        for k in range(LINE):
+            arrive(k * 2 + 1 - x, part)
+        return carry
+
+    lax.fori_loop(0, CROSS, last, 0)
+    ints_copy(rows_of(sibling), sibling, 1, sibling).wait_recv()
+    far = lax.rem(sibling + 2, 4)
+    ints_copy(rows_of(far), far, 2, sibling).wait_recv()
+    for k in range(1, 2 * LINE):
+        id_arrival(k).wait_recv()
+    for copy in locals_:
+        copy.wait()
+
+    def sent(part, carry):
+        for k in range(LINE):
+            source = k * 2 + x
+
+            @pl.when((k <= z) & (z < LINE - 1))
+            def _():
+                up(all_ref.at[source, part], source, part).wait_send()
+
+            @pl.when((k >= z) & (z > 0))
+            def _():
+                down(all_ref.at[source, part], source, part).wait_send()
+
+            @pl.when((part < CROSS) | (k == z))
+            def _():
+                over(all_ref.at[source, part], source, part).wait_send()
+
+        return carry
+
+    lax.fori_loop(0, PARTS, sent, 0)
+    for k in range(LINE):
+        source = k * 2 + 1 - x
+
+        @pl.when((k <= z) & (z < LINE - 1))
+        def _():
+            up(all_ref.at[source, CROSS], source, CROSS).wait_send()
+
+        @pl.when((k >= z) & (z > 0))
+        def _():
+            down(all_ref.at[source, CROSS], source, CROSS).wait_send()
+
+    for k in range(1, 2 * LINE):
+        id_copy(k).wait_send()
+    for index in range(3):
+        ints_copy(ints_ref, vir, index, sibling).wait_send()
+
+
+def gathered(tiles, integrals, ids):
+    targets, blocks = tiles.shape[0], integrals.shape[0]
+    anywhere = pl.BlockSpec(memory_space=pl.ANY)
+    slots = (2 * LINE, PARTS)
+    dma = pltpu.SemaphoreType.DMA
+    all_tiles, whole, all_ids = pl.pallas_call(
+        gather_kernel,
+        out_shape=[
+            jax.ShapeDtypeStruct(slots + (targets // PARTS, HALF, LANES), jnp.float32),
+            jax.ShapeDtypeStruct((blocks, 4 * integrals.shape[1], LANES), jnp.float32),
+            jax.ShapeDtypeStruct((2 * LINE, 8, LANES), jnp.int32),
+        ],
+        in_specs=[anywhere] * 3,
+        out_specs=[anywhere] * 3,
+        scratch_shapes=[dma(slots)] * 4 + [dma((2 * LINE - 1,))] * 2 + [dma((3,))] * 3,
+        compiler_params=pltpu.CompilerParams(collective_id=0, has_side_effects=True),
+    )(
+        tiles.reshape(PARTS, targets // PARTS, HALF, LANES),
+        integrals,
+        jnp.broadcast_to(jnp.pad(ids, (0, LANES - targets))[None, :], (8, LANES)),
+    )
+    return all_tiles.reshape(-1, HALF, LANES), whole, all_ids[:, 0, :targets].reshape(-1)
 
 
 def per_device(amplitudes, integrals, tile_owner, tile_key):
     targets = amplitudes.shape[0]
+    pairs = lax.axis_size("pair")
     mine = tile_owner * (NS * NS) + tile_key
-    ids = lax.all_gather(mine, "pair", axis=0, tiled=True)
-    whole = lax.all_gather(integrals, "vir", axis=0, tiled=True)
-    tiles = lax.all_gather(
-        amplitudes.reshape(targets, HALF, LANES), "pair", axis=0, tiled=True
-    )
-    whole = whole.reshape(NS * TS, NS // 2, LANES).transpose(1, 0, 2)
-    rounded = lax.reduce_precision(whole, 8, 7)
-    high = rounded.astype(jnp.bfloat16)
-    low = (whole - rounded).astype(jnp.bfloat16)
-    capacity = max(2, 2 * targets // lax.axis_size("pair"))
-    out = product(tiles, ids, mine, high, low, capacity)
+    tiles = amplitudes.reshape(targets, HALF, LANES)
+    blocked = integrals.reshape(-1, NS // 2, LANES).transpose(1, 0, 2)
+    if pairs == 2 * LINE and lax.axis_size("vir") == 4 and targets % PARTS == 0:
+        tiles, whole, ids = gathered(tiles, blocked, mine)
+    else:
+        ids = lax.all_gather(mine, "pair", axis=0, tiled=True)
+        whole = lax.all_gather(blocked, "vir", axis=1, tiled=True)
+        tiles = lax.all_gather(tiles, "pair", axis=0, tiled=True)
+    capacity = max(2, 2 * targets // pairs)
+    out = product(tiles, ids, mine, whole, capacity)
     return out.reshape(targets, TS * TS)
 
 

time: 294 us -> 173 us (0.59); the launches traced: 295 us -> 171 us
  waiting for transfers between devices: 206 us -> 0 us
  Pallas kernels: 25.8 us -> 153 us
  between operations: 14.1 us -> 0.11 us
  blocking collectives: 13.1 us -> 0 us
  local copies, waits for them, and re-layouts: 23.1 us -> 13.6 us
  other arithmetic: 13.1 us -> 4.39 us
    all_gather x2 -> x0, waiting for transfers between devices: 206 us -> none  [the longest x1 158 us: per_device(): lax.all_gather(amplitudes.reshape(targets, HALF, LANES), 'pair', axis=0,...]
    pallas_call x0 -> x1, Pallas kernels: none -> 128 us  [gathered(): pl.pallas_call(gather_kernel, out_shape=[jax.ShapeDtypeStruct(slots + (ta...]
    unnamed x1 -> x0, blocking collectives: 13.1 us -> none
    convert_element_type x1 -> x0, other arithmetic: 10.8 us -> none  [per_device(): low = (whole - rounded).astype(jnp.bfloat16)]
    reshape x1, local copies, waits for them, and re-layouts: 9.66 us -> 2 us  [per_device(): blocked = integrals.reshape(-1, NS // 2, LANES).transpose(1, 0, 2)]
    unnamed x17 -> x5, local copies, waits for them, and re-layouts: 13.4 us -> 10.8 us
  transfers between devices with their start and end apart: 2 -> 0, of which waited for: 2 -> 0; matrix products, arithmetic and copies ran while one was open for 8% -> 0% of each run, Pallas kernels for 0% -> 0%
where the time goes in v2:
time: 173 us; the launch traced here: 171 us
  Pallas kernels  153 us (88%)
  local copies, waits for them, and re-layouts  13.6 us (8%)
  other arithmetic  4.39 us (3%)
    pallas_call x1, Pallas kernels, gathered(): pl.pallas_call(gather_kernel, out_shape=[jax.ShapeDtypeStruct(slots + (ta...  128 us
    pallas_call x1, Pallas kernels, product(): pl.pallas_call(product_kernel, grid=(blocks,), out_shape=jax.ShapeDtypeSt...  24.4 us
    unnamed x5, local copies, waits for them, and re-layouts  10.8 us

profile of v2, /device:TPU:0, one launch (start us, length us, event | category | flops | bytes accessed | tf_op | source)
XLA Modules:
  0.0 171.0 jit_solution(7934643439623969768)
XLA Ops:
  0.0 0.7 fusion.3
  0.7 0.6 broadcast_in_dim.30.ids_ref
  1.3 2.8 %copy.9 = f32[12,8,32,128]{3,2,1,0:T(8,128)} copy(f32[12,8,32,128]{3,1,2,0:T(8,128)} %bitcast.26) | data formatting | bytes 3145728
  4.1 2.0 %copy.7 = f32[384,1536]{0,1:T(8,128)S(1)} copy(f32[384,1536]{1,0:T(8,128)} %param.5) | data formatting | bytes 4718592 | tf_op args[1]
  6.2 2.0 %copy.8 = f32[384,12,128]{2,0,1:T(8,128)} copy(f32[384,12,128]{0,2,1:T(8,128)S(1)} %bitcast.24) | data formatting | bytes 4718592 | tf_op jit(solution)/shard_map/reshape | solution.py:377
  8.2 128.4 %shard_map.46 = (f32[8,6,16,32,128]{4,3,2,1,0:T(8,128)}, f32[12,1536,128]{2,1,0:T(8,128)}, s32[8,8,128]{2,1,0:T(8,128)}) custom-call(f32[6,16,32,128]{3,2,1,0:T(8,128)} %bitcast.25, f32[12,384,128]{2,1,0:T(8,128)} %bitcast.23, s32[8,128]{1,0:T(8,128)} %broadcast_in_dim.30.ids_ref), custom_call_target="tpu_custom_call" | custom-call | tf_op jit(solution)/shard_map/pallas_call | solution.py:353
  136.6 0.8 compare_reduce_fusion
  137.4 0.8 remainder_reduce_fusion
  138.2 0.1 rem.62
  138.3 0.1 ne.120
  138.3 0.1 div.38
  138.4 0.2 convert_reduce_fusion.2
  138.6 0.5 convert_reduce_fusion
  139.2 0.3 select_reduce_fusion
  139.5 0.6 fusion.4
  140.2 0.1 select_reduce_fusion.1
  140.3 0.3 convert_reduce_fusion.1
  140.6 0.0 copy-start
  140.6 3.7 %copy-done = f32[12,1536,128]{2,1,0:T(8,128)S(1)} copy-done((f32[12,1536,128]{2,1,0:T(8,128)S(1)}, f32[12,1536,128]{2,1,0:T(8,128)}, u32[]{:S(2)}) %copy-start) | copy-done | bytes 9437208
  144.3 24.4 %shard_map.47 = f32[96,32,128]{2,1,0:T(8,128)S(1)} custom-call(s32[1,1,4736]{2,1,0:T(1,128)S(1)} %min.20.unit_ref, s32[1,1,96]{2,1,0:T(1,128)S(1)} %bitcast.21, s32[1,1,96]{2,1,0:T(1,128)S(1)} %bitcast.19, s32[1,1,96]{2,1,0:T(1,128)S(1)} %bitcast.20, s32[1,96]{1,0:T(1,128)S(1)} %get-tuple-element.17.home_ref, s32[1,1,896]{2,1,0:T(1,128)S(1)} %pad_bitcast_fusion.order_ref, ...), custom_call_target="tpu_custom_call" | custom-call | tf_op jit(solution)/shard_map/pallas_call | solution.py:122
  168.7 2.2 %copy.12 = f32[12,8,32,128]{3,1,2,0:T(8,128)} copy(f32[12,8,32,128]{3,2,1,0:T(8,128)S(1)} %bitcast.18) | data formatting | bytes 3145728
  (8 shorter events, 0.1 us)
Async XLA Ops:
  140.6 3.7 %copy-start = (f32[12,1536,128]{2,1,0:T(8,128)S(1)}, f32[12,1536,128]{2,1,0:T(8,128)}, u32[]{:S(2)}) copy-start(f32[12,1536,128]{2,1,0:T(8,128)} %get-tuple-element.10.whole_ref) | copy-start | bytes 28311556

commit v3 on v2

--- a/solution.py
+++ b/solution.py
@@ -12,41 +12,29 @@
 CHUNK = 4
 UNROLL = 4
 BLOCK = 768
+SCOPED = 16 * 2**20
 HALF = TS // 2
 LANES = 2 * TS
-
-
-def product_kernel(
-    unit_ref, ustart_ref, start_ref, count_ref, home_ref, order_ref, total_ref,
-    tiles_ref, whole_ref, out_ref, high_ref, low_ref,
-):
+USTART, START, END, HOME, TOTAL, UNIT = 8, 9, 10, 11, 12, 16
+
+
+def product_kernel(table_ref, tiles_ref, high_ref, low_ref, out_ref):
     left = lax.broadcasted_iota(jnp.int32, (HALF, LANES), 1) < TS
 
     @pl.when(pl.program_id(0) == 0)
     def _():
         out_ref[...] = jnp.zeros_like(out_ref)
 
-        def split(i, carry):
-            rows = pl.ds(pl.multiple_of(i * TS, TS), TS)
-            for b in range(NS // 2):
-                value = whole_ref[b, rows, :]
-                rounded = value.astype(jnp.bfloat16)
-                high_ref[b, rows, :] = rounded
-                low_ref[b, rows, :] = (value - rounded.astype(jnp.float32)).astype(jnp.bfloat16)
-            return carry
-
-        lax.fori_loop(0, NS, split, 0)
-
     def one_unit(u):
-        t = unit_ref[0, 0, u]
-        base = start_ref[0, 0, t] + CHUNK * (u - ustart_ref[0, 0, t])
-        valid = start_ref[0, 0, t] + count_ref[0, 0, t] - base
-        column = home_ref[0, t]
+        t = table_ref[0, UNIT + u // LANES, u % LANES]
+        base = table_ref[0, START, t] + CHUNK * (u - table_ref[0, USTART, t])
+        valid = table_ref[0, END, t] - base
+        column = table_ref[0, HOME, t]
         pair_block = column // 2
         tops, bottoms, highs, lows = [], [], [], []
         held = []
         for j in range(CHUNK):
-            packed = order_ref[0, 0, base + j]
+            packed = table_ref[0, (base + j) // LANES, (base + j) % LANES]
             p = packed // NS
             s = packed % NS
             tile = jnp.where(j < valid, tiles_ref[p], 0.0)
@@ -83,58 +71,62 @@
             out_ref[t] += value
         return carry
 
-    lax.fori_loop(0, (total_ref[0, 0, 0] + UNROLL - 1) // UNROLL, group, 0)
-
-
-def product(tiles, ids, mine, whole, capacity):
+    lax.fori_loop(0, (table_ref[0, TOTAL, 0] + UNROLL - 1) // UNROLL, group, 0)
+
+
+def unit_rows(targets, capacity):
+    return pl.cdiv(targets * pl.cdiv(capacity * (BLOCK // targets), CHUNK) + UNROLL, 8 * LANES) * 8
+
+
+def tables(ids, mine, capacity):
     targets = mine.shape[0]
     blocks = ids.shape[0] // BLOCK
     ids = ids.reshape(blocks, BLOCK)
     row = ids // NS
     own_row = mine // NS
     index = jnp.arange(BLOCK, dtype=jnp.int32)
-    before = (row[:, :, None] > row[:, None, :]) | (
-        (row[:, :, None] == row[:, None, :]) & (index[:, None] > index[None, :])
-    )
-    position = jnp.sum(before.astype(jnp.int32), axis=2)
+    key = row * BLOCK + index[None, :]
+    position = jnp.sum((key[:, :, None] > key[:, None, :]).astype(jnp.int32), axis=2)
     packed = index[None, :] * NS + ids % NS
+    slot = jnp.arange(8 * LANES, dtype=jnp.int32)
     order = jnp.sum(
-        jnp.where(position[:, None, :] == index[None, :, None], packed[:, None, :], 0), axis=2
-    )
-    order = jnp.pad(order, ((0, 0), (0, 128)))
+        jnp.where(position[:, None, :] == slot[None, :, None], packed[:, None, :], 0), axis=2
+    )
     start = jnp.sum((row[:, None, :] < own_row[None, :, None]).astype(jnp.int32), axis=2)
-    count = jnp.sum((row[:, None, :] == own_row[None, :, None]).astype(jnp.int32), axis=2)
-    units = (count + CHUNK - 1) // CHUNK
+    end = jnp.sum((row[:, None, :] <= own_row[None, :, None]).astype(jnp.int32), axis=2)
+    units = (end - start + CHUNK - 1) // CHUNK
     among = jnp.arange(targets, dtype=jnp.int32)
     ustart = jnp.sum(jnp.where(among[None, :, None] > among[None, None, :], units[:, None, :], 0), axis=2)
-    total = jnp.sum(units, axis=1)
-    most = targets * pl.cdiv(capacity * (BLOCK // targets), CHUNK)
-    slot = jnp.arange(most + 128, dtype=jnp.int32)
-    uend = ustart + units
+    slot = jnp.arange(unit_rows(targets, capacity) * LANES, dtype=jnp.int32)
     unit = jnp.minimum(
-        jnp.sum((uend[:, :, None] <= slot[None, None, :]).astype(jnp.int32), axis=1), targets - 1
-    )
-    smem = lambda shape: pl.BlockSpec((1, 1) + shape, lambda b: (b, 0, 0), memory_space=pltpu.SMEM)
-    tables = [unit, ustart, start, count, None, order, total[:, None]]
-    specs = [None if v is None else smem((v.shape[1],)) for v in tables]
-    tables = [(mine % NS)[None, :] if v is None else v[:, None, :] for v in tables]
-    specs[4] = pl.BlockSpec((1, targets), lambda b: (0, 0), memory_space=pltpu.SMEM)
+        jnp.sum(((ustart + units)[:, :, None] <= slot[None, None, :]).astype(jnp.int32), axis=1),
+        targets - 1,
+    )
+    home = jnp.broadcast_to((mine % NS)[None, :], start.shape)
+    total = jnp.broadcast_to(jnp.sum(units, axis=1)[:, None], start.shape)
+    figures = jnp.stack([ustart, start, end, home, total], axis=1)
+    figures = jnp.pad(figures, ((0, 0), (0, UNIT - USTART - 5), (0, LANES - targets)))
+    return jnp.concatenate(
+        [order.reshape(blocks, 8, LANES), figures, unit.reshape(blocks, -1, LANES)], axis=1
+    )
+
+
+def product(tiles, table, high, low, targets):
+    blocks = table.shape[0]
+    inside = pl.BlockSpec(memory_space=pltpu.VMEM)
     return pl.pallas_call(
         product_kernel,
         grid=(blocks,),
         out_shape=jax.ShapeDtypeStruct((targets, HALF, LANES), jnp.float32),
-        in_specs=specs
-        + [
-            pl.BlockSpec(
-                (BLOCK, HALF, LANES), lambda b: (b, 0, 0),
-                pipeline_mode=pl.Buffered(1 if blocks == 1 else 2),
-            ),
-            pl.BlockSpec(whole.shape, lambda b: (0, 0, 0), pipeline_mode=pl.Buffered(1)),
+        in_specs=[
+            pl.BlockSpec((1,) + table.shape[1:], lambda b: (b, 0, 0), memory_space=pltpu.SMEM),
+            inside if blocks == 1 else pl.BlockSpec((BLOCK, HALF, LANES), lambda b: (b, 0, 0)),
+            inside,
+            inside,
         ],
         out_specs=pl.BlockSpec((targets, HALF, LANES), lambda b: (0, 0, 0)),
-        scratch_shapes=[pltpu.VMEM(whole.shape, jnp.bfloat16)] * 2,
-        compiler_params=pltpu.CompilerParams(vmem_limit_bytes=(40 if blocks == 1 else 54) * 2**20),
-    )(*tables, tiles, whole)
+        compiler_params=pltpu.CompilerParams(vmem_limit_bytes=SCOPED if blocks == 1 else 44 * 2**20),
+    )(table, tiles, high, low)
 
 
 MESH = pl.DeviceIdType.MESH
@@ -144,7 +136,8 @@
 
 
 def gather_kernel(
-    tiles_ref, ints_ref, ids_ref, all_ref, whole_ref, allids_ref,
+    targets, tiles_ref, ints_ref, ids_ref, all_ref, high_ref, low_ref, table_ref,
+    whole_ref, allids_ref, key_ref, packed_ref, units_ref, keys, packeds, positions, unit_counts,
     up_sem, down_sem, over_sem, recv_sem, ids_send, ids_recv, ints_send, ints_recv, local_sem,
 ):
     pair = lax.axis_index("pair")
@@ -153,7 +146,7 @@
     other = pair + 1 - 2 * x
     sibling = vir + 1 - 2 * (vir % 2)
     across = lax.rem(vir + 2, 4)
-    depth = ints_ref.shape[1]
+    depth = ints_ref.shape[0]
 
     barrier = pltpu.get_barrier_semaphore()
     for k in range(1, 2 * LINE):
@@ -166,7 +159,7 @@
 
     def id_copy(k):
         return pltpu.make_async_remote_copy(
-            src_ref=ids_ref, dst_ref=allids_ref.at[pair], send_sem=ids_send.at[k - 1],
+            src_ref=ids_ref, dst_ref=allids_ref.at[pl.ds(pair, 1), :], send_sem=ids_send.at[k - 1],
             recv_sem=ids_recv.at[k - 1], device_id={"pair": lax.rem(pair + k, 2 * LINE)},
             device_id_type=MESH,
         )
@@ -174,7 +167,7 @@
     def id_arrival(k):
         source = lax.rem(pair + 2 * LINE - k, 2 * LINE)
         return pltpu.make_async_remote_copy(
-            src_ref=ids_ref, dst_ref=allids_ref.at[source], send_sem=ids_send.at[k - 1],
+            src_ref=ids_ref, dst_ref=allids_ref.at[pl.ds(source, 1), :], send_sem=ids_send.at[k - 1],
             recv_sem=ids_recv.at[k - 1], device_id={"pair": source}, device_id_type=MESH,
         )
 
@@ -227,15 +220,88 @@
         return carry
 
     lax.fori_loop(0, PARTS, own, 0)
-    ints_copy(ints_ref, vir, 0, across).start()
-    ints_copy(ints_ref, vir, 1, sibling).start()
+    for b in range(NS // 2):
+        columns = ints_ref.at[:, pl.ds(b * LANES, LANES)]
+        rows = pl.ds(pl.multiple_of(vir * depth, depth), depth)
+        pltpu.make_async_copy(columns, whole_ref.at[b, rows, :], local_sem.at[1]).start()
+        for index, peer in ((0, across), (1, sibling)):
+            pltpu.make_async_remote_copy(
+                src_ref=columns, dst_ref=whole_ref.at[b, rows, :], send_sem=ints_send.at[index],
+                recv_sem=ints_recv.at[index], device_id={"vir": peer}, device_id_type=MESH,
+            ).start()
     locals_ = [
         pltpu.make_async_copy(tiles_ref, all_ref.at[pair], local_sem.at[0]),
-        pltpu.make_async_copy(ints_ref, rows_of(vir), local_sem.at[1]),
-        pltpu.make_async_copy(ids_ref, allids_ref.at[pair], local_sem.at[2]),
+        pltpu.make_async_copy(ids_ref, allids_ref.at[pl.ds(pair, 1), :], local_sem.at[2]),
     ]
     for copy in locals_:
         copy.start()
+    locals_.pop().wait()
+    for k in range(1, 2 * LINE):
+        id_arrival(k).wait_recv()
+
+    def to_scalars(source, target):
+        copy = pltpu.make_async_copy(source, target, local_sem.at[2])
+        copy.start()
+        copy.wait()
+
+    def over_tiles(body, initial):
+        def device(d, carry):
+            return lax.fori_loop(0, targets, lambda i, c: body(d, i, c), carry, unroll=8)
+
+        return lax.fori_loop(0, 2 * LINE, device, initial)
+
+    line = lax.broadcasted_iota(jnp.int32, (8, LANES), 0)
+    lane = lax.broadcasted_iota(jnp.int32, (8, LANES), 1)
+    slot = line * LANES + lane
+    size = 8 * LANES
+    ids = allids_ref[...]
+    own_key = ids_ref[...] // NS * size
+    key = ids // NS * size + slot
+    key_ref[...] = key
+    packed_ref[...] = (line * targets + lane) * NS + ids % NS
+    to_scalars(key_ref, keys)
+    to_scalars(packed_ref, packeds)
+
+    def compare(d, i, carry):
+        position, start, end = carry
+        value = keys[d, i]
+        return (
+            position + jnp.where(value < key, 1, 0),
+            start + jnp.where(value < own_key, 1, 0),
+            end + jnp.where(value < own_key + size, 1, 0),
+        )
+
+    zero = jnp.zeros((1, LANES), jnp.int32)
+    position, start, end = over_tiles(compare, (jnp.zeros_like(key), zero, zero))
+    key_ref[...] = position
+    units = (end - start + CHUNK - 1) // CHUNK
+    units_ref[...] = units
+    to_scalars(key_ref, positions)
+    to_scalars(units_ref, unit_counts)
+
+    def place(d, i, order):
+        return order + jnp.where(slot == positions[d, i], packeds[d, i], 0)
+
+    table_ref[pl.ds(0, 8), :] = over_tiles(place, jnp.zeros_like(key))
+    rows = table_ref.shape[0] - UNIT
+    place_of = (
+        lax.broadcasted_iota(jnp.int32, (rows, LANES), 0) * LANES
+        + lax.broadcasted_iota(jnp.int32, (rows, LANES), 1)
+    )
+
+    def count(t, carry):
+        total, ustart, unit = carry
+        ustart = ustart + jnp.where(lane[:1] > t, unit_counts[0, t], 0)
+        total = total + unit_counts[0, t]
+        return total, ustart, unit + jnp.where(place_of >= total, 1, 0)
+
+    total, ustart, unit = lax.fori_loop(
+        0, targets, count, (jnp.int32(0), zero, jnp.zeros((rows, LANES), jnp.int32))
+    )
+    table_ref[pl.ds(UNIT, rows), :] = jnp.minimum(unit, targets - 1)
+    table_ref[pl.ds(USTART, UNIT - USTART), :] = jnp.concatenate(
+        [ustart, start, end, ids_ref[...] % NS, zero + total, zero, zero, zero], axis=0
+    )
 
     def from_below(distance, column, part, crosses):
         source = (z - distance) * 2 + column
@@ -295,17 +361,27 @@
     from_below(LINE - 1, 1 - x, CROSS, False)
     from_above(LINE - 1, 1 - x, CROSS, False)
 
+    ints_copy(rows_of(sibling), sibling, 1, sibling).wait_recv()
+    far = lax.rem(sibling + 2, 4)
+    ints_copy(rows_of(far), far, 2, sibling).wait_recv()
+    pltpu.make_async_copy(rows_of(vir), rows_of(vir), local_sem.at[1]).wait()
+
+    def split(i, carry):
+        rows = pl.ds(pl.multiple_of(i * TS, TS), TS)
+        for b in range(NS // 2):
+            value = whole_ref[b, rows, :]
+            rounded = value.astype(jnp.bfloat16)
+            high_ref[b, rows, :] = rounded
+            low_ref[b, rows, :] = (value - rounded.astype(jnp.float32)).astype(jnp.bfloat16)
+        return carry
+
+    lax.fori_loop(0, NS, split, 0)
     def last(part, carry):
         for k in range(LINE):
             arrive(k * 2 + 1 - x, part)
         return carry
 
     lax.fori_loop(0, CROSS, last, 0)
-    ints_copy(rows_of(sibling), sibling, 1, sibling).wait_recv()
-    far = lax.rem(sibling + 2, 4)
-    ints_copy(rows_of(far), far, 2, sibling).wait_recv()
-    for k in range(1, 2 * LINE):
-        id_arrival(k).wait_recv()
     for copy in locals_:
         copy.wait()
 
@@ -342,31 +418,41 @@
     for k in range(1, 2 * LINE):
         id_copy(k).wait_send()
     for index in range(3):
-        ints_copy(ints_ref, vir, index, sibling).wait_send()
-
-
-def gathered(tiles, integrals, ids):
-    targets, blocks = tiles.shape[0], integrals.shape[0]
+        ints_copy(rows_of(vir), vir, index, sibling).wait_send()
+
+
+def gathered(tiles, integrals, ids, capacity):
+    targets = tiles.shape[0]
+    shape = (NS // 2, NS * TS, LANES)
     anywhere = pl.BlockSpec(memory_space=pl.ANY)
+    inside = pl.BlockSpec(memory_space=pltpu.VMEM)
     slots = (2 * LINE, PARTS)
     dma = pltpu.SemaphoreType.DMA
-    all_tiles, whole, all_ids = pl.pallas_call(
-        gather_kernel,
+    all_tiles, high, low, table = pl.pallas_call(
+        functools.partial(gather_kernel, targets),
         out_shape=[
-            jax.ShapeDtypeStruct(slots + (targets // PARTS, HALF, LANES), jnp.float32),
-            jax.ShapeDtypeStruct((blocks, 4 * integrals.shape[1], LANES), jnp.float32),
-            jax.ShapeDtypeStruct((2 * LINE, 8, LANES), jnp.int32),
+            pltpu.VMEM(slots + (targets // PARTS, HALF, LANES), jnp.float32),
+            pltpu.VMEM(shape, jnp.bfloat16),
+            pltpu.VMEM(shape, jnp.bfloat16),
+            jax.ShapeDtypeStruct((UNIT + unit_rows(targets, capacity), LANES), jnp.int32),
         ],
-        in_specs=[anywhere] * 3,
-        out_specs=[anywhere] * 3,
-        scratch_shapes=[dma(slots)] * 4 + [dma((2 * LINE - 1,))] * 2 + [dma((3,))] * 3,
-        compiler_params=pltpu.CompilerParams(collective_id=0, has_side_effects=True),
+        in_specs=[anywhere, anywhere, inside],
+        out_specs=[inside] * 4,
+        scratch_shapes=[pltpu.VMEM(shape, jnp.float32)]
+        + [pltpu.VMEM((8, LANES), jnp.int32)] * 3
+        + [pltpu.VMEM((1, LANES), jnp.int32)]
+        + [pltpu.SMEM((8, LANES), jnp.int32)] * 3
+        + [pltpu.SMEM((1, LANES), jnp.int32)]
+        + [dma(slots)] * 4 + [dma((2 * LINE - 1,))] * 2 + [dma((3,))] * 3,
+        compiler_params=pltpu.CompilerParams(
+            collective_id=0, has_side_effects=True, vmem_limit_bytes=SCOPED
+        ),
     )(
         tiles.reshape(PARTS, targets // PARTS, HALF, LANES),
         integrals,
-        jnp.broadcast_to(jnp.pad(ids, (0, LANES - targets))[None, :], (8, LANES)),
-    )
-    return all_tiles.reshape(-1, HALF, LANES), whole, all_ids[:, 0, :targets].reshape(-1)
+        jnp.pad(ids, (0, LANES - targets))[None, :],
+    )
+    return all_tiles.reshape(-1, HALF, LANES), high, low, table[None]
 
 
 def per_device(amplitudes, integrals, tile_owner, tile_key):
@@ -374,15 +460,19 @@
     pairs = lax.axis_size("pair")
     mine = tile_owner * (NS * NS) + tile_key
     tiles = amplitudes.reshape(targets, HALF, LANES)
-    blocked = integrals.reshape(-1, NS // 2, LANES).transpose(1, 0, 2)
-    if pairs == 2 * LINE and lax.axis_size("vir") == 4 and targets % PARTS == 0:
-        tiles, whole, ids = gathered(tiles, blocked, mine)
+    capacity = max(2, 2 * targets // pairs)
+    if pairs == 2 * LINE and lax.axis_size("vir") == 4 and targets * pairs == BLOCK and targets % 16 == 0:
+        tiles, high, low, table = gathered(tiles, integrals, mine, capacity)
     else:
         ids = lax.all_gather(mine, "pair", axis=0, tiled=True)
-        whole = lax.all_gather(blocked, "vir", axis=1, tiled=True)
+        whole = lax.all_gather(integrals, "vir", axis=0, tiled=True)
+        whole = whole.reshape(-1, NS // 2, LANES).transpose(1, 0, 2)
         tiles = lax.all_gather(tiles, "pair", axis=0, tiled=True)
-    capacity = max(2, 2 * targets // pairs)
-    out = product(tiles, ids, mine, whole, capacity)
+        rounded = lax.reduce_precision(whole, 8, 7)
+        high = rounded.astype(jnp.bfloat16)
+        low = (whole - rounded).astype(jnp.bfloat16)
+        table = tables(ids, mine, capacity)
+    out = product(tiles, table, high, low, targets)
     return out.reshape(targets, TS * TS)
 
 

time: 173 us -> 160 us (0.925)
  local copies, waits for them, and re-layouts: 13.6 us -> 3.93 us
  other arithmetic: 4.39 us -> 0.82 us
    unnamed x5 -> x4, local copies, waits for them, and re-layouts: 10.8 us -> 3.93 us
    reduce_sum x6 -> x0, other arithmetic: 2.09 us -> none  [the longest x1 0.64 us: product(): total = jnp.sum(units, axis=1)]
    reshape x1 -> x0, local copies, waits for them, and re-layouts: 2 us -> none  [per_device(): blocked = integrals.reshape(-1, NS // 2, LANES).transpose(1, 0, 2)]
where the time goes in v3:
time: 160 us; the launch traced here: 159 us
  Pallas kernels  154 us (96%)
  local copies, waits for them, and re-layouts  3.93 us (2%)
    pallas_call x1, Pallas kernels, gathered(): pl.pallas_call(functools.partial(gather_kernel, targets), out_shape=[pltp...  128 us
    pallas_call x1, Pallas kernels, product(): pl.pallas_call(product_kernel, grid=(blocks,), out_shape=jax.ShapeDtypeSt...  25.8 us
    unnamed x4, local copies, waits for them, and re-layouts  3.93 us

profile of v3, /device:TPU:0, one launch (start us, length us, event | category | flops | bytes accessed | tf_op | source)
XLA Modules:
  0.0 158.9 jit_solution(9192817217506728613)
XLA Ops:
  0.0 0.0 copy-start
  0.0 0.8 multiply_add_fusion
  0.8 1.7 %copy.5 = f32[12,8,32,128]{3,2,1,0:T(8,128)S(1)} copy(f32[12,8,32,128]{3,1,2,0:T(8,128)} %bitcast.15) | data formatting | bytes 3145728
  2.5 0.0 copy-done
  2.5 128.3 %shard_map.46 = (f32[8,6,16,32,128]{4,3,2,1,0:T(8,128)S(1)}, bf16[12,1536,128]{2,1,0:T(8,128)(2,1)S(1)}, bf16[12,1536,128]{2,1,0:T(8,128)(2,1)S(1)}, s32[56,128]{1,0:T(8,128)S(1)}) custom-call(f32[6,16,32,128]{3,2,1,0:T(8,128)S(1)} %bitcast.12, f32[384,1536]{1,0:T(8,128)S(1)} %copy-done, s32[1,128]{1,0:T(1,128)S(1)} %pad_bitcast_fusion.ids_ref), custom_call_target="tpu_custom_call" | custom-call | tf_op jit(solution)/shard_map/pallas_call | solution.py:431
  130.9 25.8 %shard_map.47 = f32[96,32,128]{2,1,0:T(8,128)S(1)} custom-call(s32[1,56,128]{2,1,0:T(8,128)S(1)} %bitcast.14, f32[768,32,128]{2,1,0:T(8,128)S(1)} %bitcast.11, bf16[12,1536,128]{2,1,0:T(8,128)(2,1)S(1)} %get-tuple-element.11.high_ref, bf16[12,1536,128]{2,1,0:T(8,128)(2,1)S(1)} %get-tuple-element.12.low_ref), custom_call_target="tpu_custom_call" | custom-call | tf_op jit(solution)/shard_map/pallas_call | solution.py:117
  156.6 2.2 %copy.8 = f32[12,8,32,128]{3,1,2,0:T(8,128)} copy(f32[12,8,32,128]{3,2,1,0:T(8,128)S(1)} %bitcast.13) | data formatting | bytes 3145728
  (1 shorter events, 0.0 us)
Async XLA Ops:
  0.0 2.5 %copy-start = (f32[384,1536]{1,0:T(8,128)S(1)}, f32[384,1536]{1,0:T(8,128)}, u32[]{:S(2)}) copy-start(f32[384,1536]{1,0:T(8,128)} %ints_ref.1) | copy-start | bytes 7077892

commit v4 on v3

--- a/solution.py
+++ b/solution.py
@@ -10,7 +10,8 @@
 TS = 64
 NS = 24
 CHUNK = 4
-UNROLL = 4
+UNROLL = 8
+PACK = 32
 BLOCK = 768
 SCOPED = 16 * 2**20
 HALF = TS // 2
@@ -26,17 +27,17 @@
         out_ref[...] = jnp.zeros_like(out_ref)
 
     def one_unit(u):
-        t = table_ref[0, UNIT + u // LANES, u % LANES]
+        t = table_ref[0, UNIT + (u >> 7), u & (LANES - 1)]
         base = table_ref[0, START, t] + CHUNK * (u - table_ref[0, USTART, t])
         valid = table_ref[0, END, t] - base
         column = table_ref[0, HOME, t]
-        pair_block = column // 2
+        pair_block = column >> 1
         tops, bottoms, highs, lows = [], [], [], []
         held = []
         for j in range(CHUNK):
-            packed = table_ref[0, (base + j) // LANES, (base + j) % LANES]
-            p = packed // NS
-            s = packed % NS
+            packed = table_ref[0, (base + j) >> 7, (base + j) & (LANES - 1)]
+            p = packed >> 5
+            s = packed & (PACK - 1)
             tile = jnp.where(j < valid, tiles_ref[p], 0.0)
             held.append((tile, pltpu.roll(tile, TS, 1)))
             rows = pl.ds(pl.multiple_of(s * TS, TS), TS)
@@ -61,7 +62,7 @@
             lhs_high, rhs_low, preferred_element_type=jnp.float32
         )
         top, bottom = got[:HALF], got[HALF:]
-        odd = column % 2 == 1
+        odd = (column & 1) == 1
         rolled = pltpu.roll(jnp.where(odd, top, bottom), TS, 1)
         return t, jnp.where(odd, jnp.where(left, rolled, bottom), jnp.where(left, top, rolled))
 
@@ -87,7 +88,7 @@
     index = jnp.arange(BLOCK, dtype=jnp.int32)
     key = row * BLOCK + index[None, :]
     position = jnp.sum((key[:, :, None] > key[:, None, :]).astype(jnp.int32), axis=2)
-    packed = index[None, :] * NS + ids % NS
+    packed = index[None, :] * PACK + ids % NS
     slot = jnp.arange(8 * LANES, dtype=jnp.int32)
     order = jnp.sum(
         jnp.where(position[:, None, :] == slot[None, :, None], packed[:, None, :], 0), axis=2
@@ -130,9 +131,9 @@
 
 
 MESH = pl.DeviceIdType.MESH
-PARTS = 6
+PARTS = 12
 LINE = 4
-CROSS = PARTS - 1
+CROSS = PARTS - 2
 
 
 def gather_kernel(
@@ -202,7 +203,8 @@
     for k in range(1, 2 * LINE):
         id_copy(k).start()
 
-    over(tiles_ref.at[CROSS], pair, CROSS).start()
+    for part in range(CROSS, PARTS):
+        over(tiles_ref.at[part], pair, part).start()
 
     def own(part, carry):
         @pl.when(z < LINE - 1)
@@ -258,7 +260,7 @@
     own_key = ids_ref[...] // NS * size
     key = ids // NS * size + slot
     key_ref[...] = key
-    packed_ref[...] = (line * targets + lane) * NS + ids % NS
+    packed_ref[...] = (line * targets + lane) * PACK + ids % NS
     to_scalars(key_ref, keys)
     to_scalars(packed_ref, packeds)
 
@@ -339,27 +341,37 @@
             return carry
 
         lax.fori_loop(0, CROSS, step, 0)
-        from_below(distance, x, CROSS, False)
-        from_above(distance, x, CROSS, False)
-        if distance == 1:
-            arrive(other, CROSS)
+
+        def own_column(part, carry, distance=distance):
+            from_below(distance, x, part, False)
+            from_above(distance, x, part, False)
+            return carry
+
+        def other_column(part, carry, distance=distance):
+            if distance > 1:
+                from_below(distance - 1, 1 - x, part, False)
+                from_above(distance - 1, 1 - x, part, False)
+                return carry
+            arrive(other, part)
 
             @pl.when(z < LINE - 1)
             def _():
-                up(all_ref.at[other, CROSS], other, CROSS).start()
+                up(all_ref.at[other, part], other, part).start()
 
             @pl.when(z > 0)
             def _():
-                down(all_ref.at[other, CROSS], other, CROSS).start()
-
-        else:
-            from_below(distance - 1, 1 - x, CROSS, False)
-            from_above(distance - 1, 1 - x, CROSS, False)
+                down(all_ref.at[other, part], other, part).start()
+
+            return carry
+
+        lax.fori_loop(CROSS, PARTS, own_column, 0)
+        lax.fori_loop(CROSS, PARTS, other_column, 0)
         if distance == 2:
             ints_copy(rows_of(across), across, 0, across).wait_recv()
             ints_copy(rows_of(across), across, 2, sibling).start()
-    from_below(LINE - 1, 1 - x, CROSS, False)
-    from_above(LINE - 1, 1 - x, CROSS, False)
+    for part in range(CROSS, PARTS):
+        from_below(LINE - 1, 1 - x, part, False)
+        from_above(LINE - 1, 1 - x, part, False)
 
     ints_copy(rows_of(sibling), sibling, 1, sibling).wait_recv()
     far = lax.rem(sibling + 2, 4)
@@ -404,17 +416,22 @@
         return carry
 
     lax.fori_loop(0, PARTS, sent, 0)
-    for k in range(LINE):
-        source = k * 2 + 1 - x
-
-        @pl.when((k <= z) & (z < LINE - 1))
-        def _():
-            up(all_ref.at[source, CROSS], source, CROSS).wait_send()
-
-        @pl.when((k >= z) & (z > 0))
-        def _():
-            down(all_ref.at[source, CROSS], source, CROSS).wait_send()
-
+
+    def crossed(part, carry):
+        for k in range(LINE):
+            source = k * 2 + 1 - x
+
+            @pl.when((k <= z) & (z < LINE - 1))
+            def _():
+                up(all_ref.at[source, part], source, part).wait_send()
+
+            @pl.when((k >= z) & (z > 0))
+            def _():
+                down(all_ref.at[source, part], source, part).wait_send()
+
+        return carry
+
+    lax.fori_loop(CROSS, PARTS, crossed, 0)
     for k in range(1, 2 * LINE):
         id_copy(k).wait_send()
     for index in range(3):
@@ -461,7 +478,7 @@
     mine = tile_owner * (NS * NS) + tile_key
     tiles = amplitudes.reshape(targets, HALF, LANES)
     capacity = max(2, 2 * targets // pairs)
-    if pairs == 2 * LINE and lax.axis_size("vir") == 4 and targets * pairs == BLOCK and targets % 16 == 0:
+    if pairs == 2 * LINE and lax.axis_size("vir") == 4 and targets * pairs == BLOCK and targets % PARTS == 0:
         tiles, high, low, table = gathered(tiles, integrals, mine, capacity)
     else:
         ids = lax.all_gather(mine, "pair", axis=0, tiled=True)

time: 160 us -> 149 us (0.931); the launches traced: 159 us -> 150 us
  Pallas kernels: 154 us -> 145 us
    pallas_call x1, Pallas kernels: 25.8 us -> 15 us  [product(): pl.pallas_call(product_kernel, grid=(blocks,), out_shape=jax.ShapeDtypeSt...]
    pallas_call x1, Pallas kernels: 128 us -> 130 us  [gathered(): pl.pallas_call(functools.partial(gather_kernel, targets), out_shape=[pltp...]
where the time goes in v4:
time: 149 us; the launch traced here: 150 us
  Pallas kernels  145 us (97%)
  local copies, waits for them, and re-layouts  3.94 us (3%)
    pallas_call x1, Pallas kernels, gathered(): pl.pallas_call(functools.partial(gather_kernel, targets), out_shape=[pltp...  130 us
    pallas_call x1, Pallas kernels, product(): pl.pallas_call(product_kernel, grid=(blocks,), out_shape=jax.ShapeDtypeSt...  15 us
    unnamed x4, local copies, waits for them, and re-layouts  3.93 us

profile of v4, /device:TPU:0, one launch (start us, length us, event | category | flops | bytes accessed | tf_op | source)
XLA Modules:
  0.0 150.1 jit_solution(16272657390962085369)
XLA Ops:
  0.0 0.0 copy-start
  0.0 0.8 multiply_add_fusion
  0.8 1.7 %copy.10 = f32[12,8,32,128]{3,2,1,0:T(8,128)S(1)} copy(f32[12,8,32,128]{3,1,2,0:T(8,128)} %bitcast.16) | data formatting | bytes 3145728
  2.5 0.0 copy-done
  2.5 130.3 %shard_map.46 = (f32[8,12,8,32,128]{4,3,2,1,0:T(8,128)S(1)}, bf16[12,1536,128]{2,1,0:T(8,128)(2,1)S(1)}, bf16[12,1536,128]{2,1,0:T(8,128)(2,1)S(1)}, s32[56,128]{1,0:T(8,128)S(1)}) custom-call(f32[12,8,32,128]{3,2,1,0:T(8,128)S(1)} %copy.10, f32[384,1536]{1,0:T(8,128)S(1)} %copy-done, s32[1,128]{1,0:T(1,128)S(1)} %pad_bitcast_fusion.ids_ref), custom_call_target="tpu_custom_call" | custom-call | tf_op jit(solution)/shard_map/pallas_call | solution.py:448
  132.9 15.0 %shard_map.47 = f32[96,32,128]{2,1,0:T(8,128)S(1)} custom-call(s32[1,56,128]{2,1,0:T(8,128)S(1)} %bitcast.15, f32[768,32,128]{2,1,0:T(8,128)S(1)} %bitcast.13, bf16[12,1536,128]{2,1,0:T(8,128)(2,1)S(1)} %get-tuple-element.11.high_ref, bf16[12,1536,128]{2,1,0:T(8,128)(2,1)S(1)} %get-tuple-element.12.low_ref), custom_call_target="tpu_custom_call" | custom-call | tf_op jit(solution)/shard_map/pallas_call | solution.py:118
  147.9 2.2 %copy.9 = f32[12,8,32,128]{3,1,2,0:T(8,128)} copy(f32[12,8,32,128]{3,2,1,0:T(8,128)S(1)} %bitcast.14) | data formatting | bytes 3145728
  (1 shorter events, 0.0 us)
Async XLA Ops:
  0.0 2.5 %copy-start = (f32[384,1536]{1,0:T(8,128)S(1)}, f32[384,1536]{1,0:T(8,128)}, u32[]{:S(2)}) copy-start(f32[384,1536]{1,0:T(8,128)} %ints_ref.1) | copy-start | bytes 7077892

commit v5 on v4

--- a/solution.py
+++ b/solution.py
@@ -10,7 +10,7 @@
 TS = 64
 NS = 24
 CHUNK = 4
-UNROLL = 8
+UNROLL = 16
 PACK = 32
 BLOCK = 768
 SCOPED = 16 * 2**20
@@ -131,9 +131,9 @@
 
 
 MESH = pl.DeviceIdType.MESH
-PARTS = 12
+PARTS = 6
 LINE = 4
-CROSS = PARTS - 2
+CROSS = PARTS - 1
 
 
 def gather_kernel(

time: 149 us -> 146 us (0.980)
  Pallas kernels: 145 us -> 141 us
    pallas_call x1, Pallas kernels: 15 us -> 12.6 us  [product(): pl.pallas_call(product_kernel, grid=(blocks,), out_shape=jax.ShapeDtypeSt...]
    pallas_call x1, Pallas kernels: 130 us -> 128 us  [gathered(): pl.pallas_call(functools.partial(gather_kernel, targets), out_shape=[pltp...]
where the time goes in v5:
time: 146 us
  Pallas kernels  141 us (97%)
  local copies, waits for them, and re-layouts  3.93 us (3%)
    pallas_call x1, Pallas kernels, gathered(): pl.pallas_call(functools.partial(gather_kernel, targets), out_shape=[pltp...  128 us
    pallas_call x1, Pallas kernels, product(): pl.pallas_call(product_kernel, grid=(blocks,), out_shape=jax.ShapeDtypeSt...  12.6 us
    unnamed x4, local copies, waits for them, and re-layouts  3.93 us

profile of v5, /device:TPU:0, one launch (start us, length us, event | category | flops | bytes accessed | tf_op | source)
XLA Modules:
  0.0 145.7 jit_solution(10545914912977905757)
XLA Ops:
  0.0 0.0 copy-start
  0.0 0.8 multiply_add_fusion
  0.8 1.7 %copy.5 = f32[12,8,32,128]{3,2,1,0:T(8,128)S(1)} copy(f32[12,8,32,128]{3,1,2,0:T(8,128)} %bitcast.15) | data formatting | bytes 3145728
  2.5 0.0 copy-done
  2.5 128.3 %shard_map.46 = (f32[8,6,16,32,128]{4,3,2,1,0:T(8,128)S(1)}, bf16[12,1536,128]{2,1,0:T(8,128)(2,1)S(1)}, bf16[12,1536,128]{2,1,0:T(8,128)(2,1)S(1)}, s32[56,128]{1,0:T(8,128)S(1)}) custom-call(f32[6,16,32,128]{3,2,1,0:T(8,128)S(1)} %bitcast.12, f32[384,1536]{1,0:T(8,128)S(1)} %copy-done, s32[1,128]{1,0:T(1,128)S(1)} %pad_bitcast_fusion.ids_ref), custom_call_target="tpu_custom_call" | custom-call | tf_op jit(solution)/shard_map/pallas_call | solution.py:448
  130.9 12.6 %shard_map.47 = f32[96,32,128]{2,1,0:T(8,128)S(1)} custom-call(s32[1,56,128]{2,1,0:T(8,128)S(1)} %bitcast.14, f32[768,32,128]{2,1,0:T(8,128)S(1)} %bitcast.11, bf16[12,1536,128]{2,1,0:T(8,128)(2,1)S(1)} %get-tuple-element.11.high_ref, bf16[12,1536,128]{2,1,0:T(8,128)(2,1)S(1)} %get-tuple-element.12.low_ref), custom_call_target="tpu_custom_call" | custom-call | tf_op jit(solution)/shard_map/pallas_call | solution.py:118
  143.4 2.2 %copy.8 = f32[12,8,32,128]{3,1,2,0:T(8,128)} copy(f32[12,8,32,128]{3,2,1,0:T(8,128)S(1)} %bitcast.13) | data formatting | bytes 3145728
  (1 shorter events, 0.0 us)
Async XLA Ops:
  0.0 2.5 %copy-start = (f32[384,1536]{1,0:T(8,128)S(1)}, f32[384,1536]{1,0:T(8,128)}, u32[]{:S(2)}) copy-start(f32[384,1536]{1,0:T(8,128)} %ints_ref.1) | copy-start | bytes 7077892
